TPU v7x, 32 devices: a whole 2x2x4 slice. The times are simulated.
32 devices in a mesh: rec: 2 (over y), leaf: 4 (over z), rhs: 2 (over x), pan: 2 (over core).
Axes of the slice: x: 2, y: 2, z: 4, core: 2. Of those that a mesh axis runs over, the one named last changes fastest.
Arguments:
- bottom_source: bfloat16 [32768, 256], P(('rec', 'leaf', 'rhs', 'pan')), parts along dimension 0, may hold values from -6 to 6
- bottom_inverse: bfloat16 [32768, 1024], P(('rec', 'leaf', 'rhs', 'pan')), parts along dimension 0, as said below
- bottom_update: bfloat16 [4096, 1024], P(('rec', 'leaf', 'rhs', 'pan')), parts along dimension 0, may hold values from -0.0625 to 0.0625
- bottom_sensitivity: bfloat16 [1024, 16384], P('rec', ('leaf', 'rhs', 'pan')), parts along dimension 0, may hold values from -0.03125 to 0.03125
- bottom_order: int32 [16, 1024], P(('leaf', 'rhs', 'pan')), may hold values from 0 to 1023, each once within a row
- bottom_extent: int32 [16], P(('leaf', 'rhs', 'pan')), may hold values from 384 to 1024, as said below
- bottom_targets: int32 [16, 128], P(('leaf', 'rhs', 'pan')), may hold values from 0 to 255, as said below
- upper_source: bfloat16 [3584, 256], P(('rec', 'leaf'), ('rhs', 'pan')), parts along dimension 0, may hold values from -6 to 6
- upper_inverse: bfloat16 [3584, 256], P(('rec', 'leaf')), parts along dimension 0, as said below
- upper_update: bfloat16 [256, 1536], P('rec', 'leaf'), parts along dimension 0, may hold values from -0.25 to 0.25
- upper_targets: int32 [6, 128], replicated, may hold values from 0 to 255, as said below
Outputs:
- adjoint: bfloat16 [32768, 256], P(('rec', 'leaf', 'rhs', 'pan')), parts along dimension 0
- gradient: float32 [1024, 256], P(('rec', 'leaf', 'rhs', 'pan')), parts along dimension 0
There are 2 independent parts, one for each index of `rec`. A program takes and returns all parts, laid end to end along the dimension named above; an argument that names none is the same for every part. Nothing has to cross between parts.
Inputs may be any that keep to these rules, and one draw needn't show every extreme that they name: `bottom_inverse`: lower triangular, with its diagonal between 0.6 and 1.4. `upper_inverse`: lower triangular in each front's row order, with its diagonal between 0.6 and 1.4. `bottom_extent`: a multiple of 128; some front uses all 1024 rows. `bottom_targets`: the rows of one front go to distinct rows. `upper_targets`: the rows of one front go to distinct rows.
All inputs are finite; a program needn't handle non-finite values.
Results may differ from a plain program's by a relative error of at most 0.0058.
Values may be sent and summed in bfloat16 or wider, within the bound.
A program may use at most 64 MiB of HBM per device.

v0:
```python
import jax
import jax.numpy as jnp
from jax import lax
from jax.sharding import PartitionSpec as P


def partner(value, axis, apart):
    mask = 2**apart
    pairs = [(source, source ^ mask) for source in range(lax.axis_size(axis))]
    return lax.ppermute(value, axis, pairs)


def climb_sum(values, bit_count):
    for bit_index in range(bit_count):
        values = values + partner(values, "leaf", bit_index)
    return values


def descend_sum(values, bit_count):
    for bit_index in range(bit_count):
        values = values + partner(values, "leaf", bit_index)
    return values


def shards(
    bottom_source,
    bottom_inverse,
    bottom_update,
    bottom_sensitivity,
    bottom_order,
    bottom_extent,
    bottom_targets,
    upper_source,
    upper_inverse,
    upper_update,
    upper_targets,
):
    leaves = lax.axis_size("leaf")
    depth = leaves.bit_length() - 1
    leaf_place = lax.axis_index("leaf")
    front_rows = bottom_inverse.shape[0]
    front_size = upper_inverse.shape[1]
    order_rows = bottom_order[0]
    row_mask = (jnp.arange(front_rows, dtype=jnp.int32) < bottom_extent[0]).astype(jnp.bfloat16)[
        :, None
    ]
    ordered = bottom_source[order_rows] * row_mask
    solved = (
        jnp.dot(bottom_inverse, ordered, preferred_element_type=jnp.float32) * row_mask
    ).astype(jnp.bfloat16)
    contrib = jnp.dot(bottom_update, solved, preferred_element_type=jnp.float32)
    spread = (
        jnp.zeros((front_size, contrib.shape[1]), jnp.float32).at[bottom_targets[0]].set(contrib)
    )
    summed = lax.psum(spread, ("rhs", "pan"))
    loads = lax.all_gather(upper_source, ("rhs", "pan"), axis=1, tiled=True)
    column_count = summed.shape[1]
    front_input = (loads[0:front_size].astype(jnp.float32) - summed).astype(jnp.bfloat16)
    solved_upper = []
    for height in range(depth + 1):
        row_count = front_size >> height
        offset = 2 * front_size - (2 * front_size >> height)
        inverse_now = upper_inverse[offset : offset + row_count]
        solved_front = jnp.dot(inverse_now, front_input, preferred_element_type=jnp.float32).astype(
            jnp.bfloat16
        )
        solved_upper.append(solved_front)
        if height < depth:
            update_now = upper_update[:, offset : offset + row_count]
            lifted = jnp.dot(update_now, solved_front, preferred_element_type=jnp.float32)
            map_row = 2 * leaves - (2 * leaves >> height) + leaf_place // (1 << height)
            targets = lax.dynamic_slice_in_dim(upper_targets, map_row, 1, 0)[0]
            partial_input = (
                jnp.zeros((front_size, column_count), jnp.float32).at[targets].set(-lifted)
            )
            parent_rows = front_size >> height + 1
            parent_offset = 2 * front_size - (2 * front_size >> height + 1)
            parent_place = leaf_place % (2 << height) * parent_rows
            own_load = loads[parent_offset : parent_offset + parent_rows].astype(jnp.float32)
            current = lax.dynamic_slice_in_dim(partial_input, parent_place, parent_rows, 0)
            partial_input = lax.dynamic_update_slice_in_dim(
                partial_input, current + own_load, parent_place, 0
            )
            front_input = climb_sum(partial_input, height + 1).astype(jnp.bfloat16)
    back_rows = None
    for height in range(depth, -1, -1):
        row_count = front_size >> height
        offset = 2 * front_size - (2 * front_size >> height)
        inverse_now = upper_inverse[offset : offset + row_count]
        if height == depth:
            residue = solved_upper[height]
        else:
            map_row = 2 * leaves - (2 * leaves >> height) + leaf_place // (1 << height)
            targets = lax.dynamic_slice_in_dim(upper_targets, map_row, 1, 0)[0]
            picked = back_rows[targets]
            update_now = upper_update[:, offset : offset + row_count]
            coupled = jnp.einsum(
                "rj,rc->jc", update_now, picked, preferred_element_type=jnp.float32
            )
            residue = (solved_upper[height].astype(jnp.float32) - coupled).astype(jnp.bfloat16)
        partial_back = jnp.einsum(
            "ij,ic->jc", inverse_now, residue, preferred_element_type=jnp.float32
        )
        back_rows = descend_sum(partial_back, height).astype(jnp.bfloat16)
    picked_root = back_rows[bottom_targets[0]]
    coupled_root = jnp.einsum(
        "rj,rc->jc", bottom_update, picked_root, preferred_element_type=jnp.float32
    )
    bottom_residue = ((solved.astype(jnp.float32) - coupled_root) * row_mask).astype(jnp.bfloat16)
    bottom_back = (
        jnp.einsum("ij,ic->jc", bottom_inverse, bottom_residue, preferred_element_type=jnp.float32)
        * row_mask
    ).astype(jnp.bfloat16)
    adjoint = jnp.zeros_like(bottom_back).at[order_rows].set(bottom_back)
    gradient = lax.psum_scatter(
        -jnp.dot(bottom_sensitivity, adjoint, preferred_element_type=jnp.float32),
        ("leaf", "rhs", "pan"),
        scatter_dimension=0,
        tiled=True,
    )
    return (adjoint, gradient)


def solution(mesh):
    placed = (
        P(("rec", "leaf", "rhs", "pan"), None),
        P(("rec", "leaf", "rhs", "pan"), None),
        P(("rec", "leaf", "rhs", "pan"), None),
        P("rec", ("leaf", "rhs", "pan")),
        P(("leaf", "rhs", "pan"), None),
        P(("leaf", "rhs", "pan")),
        P(("leaf", "rhs", "pan"), None),
        P(("rec", "leaf"), ("rhs", "pan")),
        P(("rec", "leaf"), None),
        P("rec", "leaf"),
        P(),
    )
    return jax.shard_map(
        shards,
        mesh=mesh,
        in_specs=placed,
        out_specs=(P(("rec", "leaf", "rhs", "pan"), None), P(("rec", "leaf", "rhs", "pan"), None)),
        check_vma=False,
    )
```

profile of v0, /device:TPU:0, one launch (start us, length us, event | category | flops | bytes accessed | tf_op | source)
XLA Modules:
  0.0 189.3 jit_solution(15696807839329698646)
XLA Ops:
  8.0 0.7 fusion.43
  8.7 0.7 compare_select_fusion
  9.4 4.6 %gather_fusion = bf16[1024,256]{1,0:T(8,128)(2,1)S(1)} fusion(bf16[1024,256]{1,0:T(8,128)(2,1)} %param.11, s32[1024]{0:T(1024)S(1)} %broadcast_clamp_fusion), kind=kCustom, calls=%fused_computation | custom fusion | bytes 1052672 | tf_op jit(solution)/shard_map/gather | solution.py:47
  14.0 1.0 fusion.3
  15.0 0.8 copy-done.3
  15.8 0.3 convolution_bitcast_fusion.2
  16.1 0.1 copy.28
  16.2 1.7 scatter_custom_fusion
  18.0 7.2 %all_gather.3 = bf16[448,256]{0,1:T(8,128)(2,1)S(1)} all-gather(bf16[448,64]{0,1:T(8,128)(2,1)S(1)} %copy-done.7), channel_id=1, replica_groups=mesh['rec'=2,'leaf'=4,'rhs'=2,'pan'=2] {'rhs','pan'}, dimensions={1}, use_global_device_ids=true | all-gather | bytes 286720 | tf_op jit(solution)/shard_map/all_gather | solution.py:56
  25.3 0.1 copy.41
  25.4 0.1 copy.40
  25.5 0.8 fusion.45
  26.3 26.5 %all-reduce.2.cloned.1.call-done = f32[256,256]{1,0:T(8,128)} async-done(((f32[256,256]{1,0:T(8,128)}), f32[256,256]{1,0:T(8,128)}) %all-reduce.2.cloned.1.call-update) | async-done | bytes 262160 | tf_op jit(solution)/shard_map/psum | solution.py:55
  52.8 1.2 convolution_convert_fusion.1
  53.9 0.2 fusion.8
  54.1 0.1 copy.29
  54.2 1.1 scatter_custom_fusion.1
  55.4 1.6 collective-permute-start
  57.0 5.1 %collective-permute-done = f32[256,256]{1,0:T(8,128)S(1)} collective-permute-done((f32[256,256]{1,0:T(8,128)S(1)}, f32[256,256]{1,0:T(8,128)S(1)}, u32[]{:S(2)}, u32[]{:S(2)}) %collective-permute-start) | collective-permute-done | bytes 262176 | tf_op jit(solution)/shard_map/ppermute | solution.py:10
  62.1 0.2 convolution_convert_fusion.2
  62.3 0.2 fusion.9
  62.5 0.1 copy.31
  62.6 1.1 scatter_custom_fusion.2
  63.7 1.8 collective-permute-start.1
  65.5 4.6 %collective-permute-done.1 = f32[256,256]{1,0:T(8,128)S(1)} collective-permute-done((f32[256,256]{1,0:T(8,128)S(1)}, f32[256,256]{1,0:T(8,128)S(1)}, u32[]{:S(2)}, u32[]{:S(2)}) %collective-permute-start.1) | collective-permute-done | bytes 262176 | tf_op jit(solution)/shard_map/ppermute | solution.py:10
  70.2 3.3 %collective-permute-start.2 = (f32[256,256]{1,0:T(8,128)S(1)}, f32[256,256]{1,0:T(8,128)S(1)}, u32[]{:S(2)}, u32[]{:S(2)}) collective-permute-start(f32[256,256]{1,0:T(8,128)S(1)} %add.117), channel_id=1, source_target_pairs={{0,8},{4,12},{8,0},{12,4},{1,9},{5,13},{9,1},{13,5},{2,10},{6,14},... | collective-permute-start | bytes 786440 | tf_op jit(solution)/shard_map/ppermute | solution.py:10
  73.5 8.1 %collective-permute-done.2 = f32[256,256]{1,0:T(8,128)S(1)} collective-permute-done((f32[256,256]{1,0:T(8,128)S(1)}, f32[256,256]{1,0:T(8,128)S(1)}, u32[]{:S(2)}, u32[]{:S(2)}) %collective-permute-start.2) | collective-permute-done | bytes 262176 | tf_op jit(solution)/shard_map/ppermute | solution.py:10
  81.6 0.4 convolution_bitcast_fusion.1
  82.0 0.8 collective-permute-start.3
  82.8 5.6 %collective-permute-done.3 = f32[256,256]{0,1:T(8,128)S(1)} collective-permute-done((f32[256,256]{0,1:T(8,128)S(1)}, f32[256,256]{0,1:T(8,128)S(1)}, u32[]{:S(2)}, u32[]{:S(2)}) %collective-permute-start.3) | collective-permute-done | bytes 262176 | tf_op jit(solution)/shard_map/ppermute | solution.py:10
  88.5 2.8 %collective-permute-start.4 = (f32[256,256]{0,1:T(8,128)S(1)}, f32[256,256]{0,1:T(8,128)S(1)}, u32[]{:S(2)}, u32[]{:S(2)}) collective-permute-start(f32[256,256]{0,1:T(8,128)S(1)} %add.119), channel_id=1, source_target_pairs={{0,8},{4,12},{8,0},{12,4},{1,9},{5,13},{9,1},{13,5},{2,10},{6,14},... | collective-permute-start | bytes 786440 | tf_op jit(solution)/shard_map/ppermute | solution.py:10
  91.3 9.9 %collective-permute-done.4 = f32[256,256]{0,1:T(8,128)S(1)} collective-permute-done((f32[256,256]{0,1:T(8,128)S(1)}, f32[256,256]{0,1:T(8,128)S(1)}, u32[]{:S(2)}, u32[]{:S(2)}) %collective-permute-start.4) | collective-permute-done | bytes 262176 | tf_op jit(solution)/shard_map/ppermute | solution.py:10
  101.2 0.1 copy.33
  101.3 0.8 gather_fusion.1
  102.2 1.1 convolution_bitcast_fusion
  103.3 0.8 collective-permute-start.5
  104.1 6.5 %collective-permute-done.5 = f32[256,256]{0,1:T(8,128)S(1)} collective-permute-done((f32[256,256]{0,1:T(8,128)S(1)}, f32[256,256]{0,1:T(8,128)S(1)}, u32[]{:S(2)}, u32[]{:S(2)}) %collective-permute-start.5) | collective-permute-done | bytes 262176 | tf_op jit(solution)/shard_map/ppermute | solution.py:10
  110.7 0.1 copy.34
  110.8 0.8 gather_fusion.2
  111.6 1.2 fusion.7
  112.8 0.1 copy.35
  112.9 0.8 gather_fusion.3
  113.8 1.8 fusion.4
  115.6 0.2 copy.36
  115.8 5.1 %scatter_custom_fusion.3 = bf16[1024,256]{1,0:T(8,128)(2,1)S(1)} fusion(s32[1024]{0:T(1024)S(1)} %bitcast.59, bf16[1024,256]{1,0:T(8,128)(2,1)S(1)} %copy.36, bf16[]{:T(256)} %constant.56.clone.1), kind=kCustom, calls=%fused_computation.42 | custom fusion | bytes 524290 | tf_op jit(solution)/shard_map/scatter | solution.py:114
  120.9 1.9 %fusion.5 = f32[512,256]{0,1:T(8,128)S(1)} fusion(bf16[1024,256]{1,0:T(8,128)(2,1)S(1)} %scatter_custom_fusion.3, bf16[512,1024]{1,0:T(8,128)(2,1)} %param.14), kind=kOutput, calls=%fused_computation.17 | convolution fusion | flops 268566528 | bytes 2097152 | tf_op jit(solution)/shard_map/dot_general | solution.py:116
  122.8 1.0 copy.38
  123.9 58.6 %reduce-scatter.4.cloned.1.call-done = f32[32,256]{1,0:T(8,128)} async-done(((f32[512,256]{1,0:T(8,128)}), f32[32,256]{1,0:T(8,128)}) %reduce-scatter.4.cloned.1.call-update) | async-done | bytes 32784
  (34 shorter events, 0.5 us)
Async XLA Ops:
  7.2 6.8 %copy-start = (bf16[1024,1024]{1,0:T(8,128)(2,1)S(1)}, bf16[1024,1024]{1,0:T(8,128)(2,1)}, u32[]{:S(2)}) copy-start(bf16[1024,1024]{1,0:T(8,128)(2,1)} %param.12) | copy-start | bytes 6291460
  7.2 45.6 %all-reduce.2.cloned.1.call-start = ((), (), s32[]{:S(2)}) async-start(), calls=%async_computation.1 | async-start | bytes 524288 | tf_op jit(solution)/shard_map/psum | solution.py:55
  14.0 1.8 copy-start.6
  14.0 4.0 %copy-start.7 = (bf16[448,64]{0,1:T(8,128)(2,1)S(1)}, bf16[448,64]{0,1:T(8,128)(2,1)}, u32[]{:S(2)}) copy-start(bf16[448,64]{0,1:T(8,128)(2,1)} %param.18) | copy-start | bytes 172036
  15.0 0.8 copy-start.3
  15.8 36.9 %copy-start.2 = (bf16[448,256]{1,0:T(8,128)(2,1)S(1)}, bf16[448,256]{1,0:T(8,128)(2,1)}, u32[]{:S(2)}) copy-start(bf16[448,256]{1,0:T(8,128)(2,1)} %param.19) | copy-start | bytes 688132
  15.8 38.1 %copy-start.5 = (bf16[128,384]{1,0:T(8,128)(2,1)S(1)}, bf16[128,384]{1,0:T(8,128)(2,1)}, u32[]{:S(2)}) copy-start(bf16[128,384]{1,0:T(8,128)(2,1)} %param.20) | copy-start | bytes 294916
  17.9 164.5 %reduce-scatter.4.cloned.1.call-start = ((), (), s32[]{:S(2)}) async-start(), calls=%async_computation.2 | async-start | bytes 557056
  55.4 6.7 %collective-permute-start = (f32[256,256]{1,0:T(8,128)S(1)}, f32[256,256]{1,0:T(8,128)S(1)}, u32[]{:S(2)}, u32[]{:S(2)}) collective-permute-start(f32[256,256]{1,0:T(8,128)S(1)} %add_dynamic-update-slice_fusion), channel_id=1, source_target_pairs={{0,4},{4,0},{8,12},{12,8},{1,5},{5,1},{9,13},{13,9},{2,6},{6,2},{1... | collective-permute-start | bytes 786440 | tf_op jit(solution)/shard_map/ppermute | solution.py:10
  63.7 6.4 %collective-permute-start.1 = (f32[256,256]{1,0:T(8,128)S(1)}, f32[256,256]{1,0:T(8,128)S(1)}, u32[]{:S(2)}, u32[]{:S(2)}) collective-permute-start(f32[256,256]{1,0:T(8,128)S(1)} %add_dynamic-update-slice_fusion.1), channel_id=1, source_target_pairs={{0,4},{4,0},{8,12},{12,8},{1,5},{5,1},{9,13},{13,9},{2,6},{6,2},{1... | collective-permute-start | bytes 786440 | tf_op jit(solution)/shard_map/ppermute | solution.py:10
  70.2 11.4 %collective-permute-start.2 = (f32[256,256]{1,0:T(8,128)S(1)}, f32[256,256]{1,0:T(8,128)S(1)}, u32[]{:S(2)}, u32[]{:S(2)}) collective-permute-start(f32[256,256]{1,0:T(8,128)S(1)} %add.117), channel_id=1, source_target_pairs={{0,8},{4,12},{8,0},{12,4},{1,9},{5,13},{9,1},{13,5},{2,10},{6,14},... | collective-permute-start | bytes 786440 | tf_op jit(solution)/shard_map/ppermute | solution.py:10
  82.0 6.4 %collective-permute-start.3 = (f32[256,256]{0,1:T(8,128)S(1)}, f32[256,256]{0,1:T(8,128)S(1)}, u32[]{:S(2)}, u32[]{:S(2)}) collective-permute-start(f32[256,256]{0,1:T(8,128)S(1)} %convolution_bitcast_fusion.1), channel_id=1, source_target_pairs={{0,4},{4,0},{8,12},{12,8},{1,5},{5,1},{9,13},{13,9},{2,6},{6,2},{1... | collective-permute-start | bytes 786440 | tf_op jit(solution)/shard_map/ppermute | solution.py:10
  88.5 12.7 %collective-permute-start.4 = (f32[256,256]{0,1:T(8,128)S(1)}, f32[256,256]{0,1:T(8,128)S(1)}, u32[]{:S(2)}, u32[]{:S(2)}) collective-permute-start(f32[256,256]{0,1:T(8,128)S(1)} %add.119), channel_id=1, source_target_pairs={{0,8},{4,12},{8,0},{12,4},{1,9},{5,13},{9,1},{13,5},{2,10},{6,14},... | collective-permute-start | bytes 786440 | tf_op jit(solution)/shard_map/ppermute | solution.py:10
  101.2 12.6 %copy-start.4 = (bf16[256,1024]{1,0:T(8,128)(2,1)S(1)}, bf16[256,1024]{1,0:T(8,128)(2,1)}, u32[]{:S(2)}) copy-start(bf16[256,1024]{1,0:T(8,128)(2,1)} %copy-done.3) | copy-start | bytes 1572868
  103.3 7.3 %collective-permute-start.5 = (f32[256,256]{0,1:T(8,128)S(1)}, f32[256,256]{0,1:T(8,128)S(1)}, u32[]{:S(2)}, u32[]{:S(2)}) collective-permute-start(f32[256,256]{0,1:T(8,128)S(1)} %convolution_bitcast_fusion), channel_id=1, source_target_pairs={{0,4},{4,0},{8,12},{12,8},{1,5},{5,1},{9,13},{13,9},{2,6},{6,2},{1... | collective-permute-start | bytes 786440 | tf_op jit(solution)/shard_map/ppermute | solution.py:10
  120.9 61.5 %copy-start.1 = (bf16[1024,256]{1,0:T(8,128)(2,1)}, bf16[1024,256]{1,0:T(8,128)(2,1)S(1)}, u32[]{:S(2)}) copy-start(bf16[1024,256]{1,0:T(8,128)(2,1)S(1)} %scatter_custom_fusion.3) | copy-start | bytes 1572868
Sparse Core Ops, SparseCore 0:
  18.1 34.6 all-reduce.1
  124.0 58.4 reduce-scatter.3
where the time goes:
time: 190 us; the launch traced here: 189 us
  waiting for transfers between devices  125 us (66%)
  local copies, waits for them, and re-layouts  19 us (10%)
  between operations  15.2 us (8%)
  starting transfers between devices  11.1 us (6%)
  matrix products  9.46 us (5%)
  blocking collectives  7.19 us (4%)
  other arithmetic  2.34 us (1%)
    unnamed x3, waiting for transfers between devices  58.6 us
    ppermute x6, waiting for transfers between devices, partner(): return lax.ppermute(value, axis, pairs)  39.9 us
    psum x1, waiting for transfers between devices, shards(): summed = lax.psum(spread, ('rhs', 'pan'))  26.5 us
    ppermute x6, starting transfers between devices, partner(): return lax.ppermute(value, axis, pairs)  11 us
    all_gather x1, blocking collectives, shards(): loads = lax.all_gather(upper_source, ('rhs', 'pan'), axis=1, tiled=True)  7.19 us
    scatter x1, local copies, waits for them, and re-layouts, shards(): adjoint = jnp.zeros_like(bottom_back).at[order_rows].set(bottom_back)  5.07 us
    gather x1, local copies, waits for them, and re-layouts, shards(): ordered = bottom_source[order_rows] * row_mask  4.57 us
  transfers between devices with their start and end apart: 8, of which 8 were waited for; matrix products, arithmetic and copies ran while one was open for 1% of the time, Pallas kernels for 0%

commit v1 on v0

--- a/solution.py
+++ b/solution.py
@@ -1,7 +1,15 @@
+import functools
 import jax
 import jax.numpy as jnp
 from jax import lax
 from jax.sharding import PartitionSpec as P
+
+
+def view_loads(x_local, which_axis):
+    return jnp.sum(jax.lax.all_gather(x_local, which_axis), axis=0)
+
+
+joints_order = functools.partial(view_loads, which_axis=("rhs", "pan"))
 
 
 def partner(value, axis, apart):
@@ -52,7 +60,7 @@
     spread = (
         jnp.zeros((front_size, contrib.shape[1]), jnp.float32).at[bottom_targets[0]].set(contrib)
     )
-    summed = lax.psum(spread, ("rhs", "pan"))
+    summed = joints_order(spread)
     loads = lax.all_gather(upper_source, ("rhs", "pan"), axis=1, tiled=True)
     column_count = summed.shape[1]
     front_input = (loads[0:front_size].astype(jnp.float32) - summed).astype(jnp.bfloat16)

time: 190 us -> 181 us (0.953)
  waiting for transfers between devices: 125 us -> 118 us
    psum x1 -> x0, waiting for transfers between devices: 26.5 us -> none  [shards(): summed = lax.psum(spread, ('rhs', 'pan'))]
    all_gather x0 -> x1, waiting for transfers between devices: none -> 12 us  [view_loads(): return jnp.sum(jax.lax.all_gather(x_local, which_axis), axis=0)]
    ppermute x6, waiting for transfers between devices: 39.9 us -> 48.7 us  [partner(): return lax.ppermute(value, axis, pairs)]
  transfers between devices with their start and end apart: 8 -> 8, of which waited for: 8 -> 8; matrix products, arithmetic and copies ran while one was open for 1% -> 0% of each run, Pallas kernels for 0% -> 0%
where the time goes in v1:
time: 181 us
  waiting for transfers between devices  118 us (65%)
  local copies, waits for them, and re-layouts  20 us (11%)
  between operations  15.2 us (8%)
  starting transfers between devices  10.2 us (6%)
  matrix products  7.71 us (4%)
  blocking collectives  7.19 us (4%)
  other arithmetic  3.01 us (2%)
    unnamed x3, waiting for transfers between devices  57 us
    ppermute x6, waiting for transfers between devices, partner(): return lax.ppermute(value, axis, pairs)  48.7 us
    all_gather x1, waiting for transfers between devices, view_loads(): return jnp.sum(jax.lax.all_gather(x_local, which_axis), axis=0)  12 us
    ppermute x6, starting transfers between devices, partner(): return lax.ppermute(value, axis, pairs)  10.1 us
    all_gather x1, blocking collectives, shards(): loads = lax.all_gather(upper_source, ('rhs', 'pan'), axis=1, tiled=True)  7.19 us
    scatter x1, local copies, waits for them, and re-layouts, shards(): adjoint = jnp.zeros_like(bottom_back).at[order_rows].set(bottom_back)  5.07 us
    gather x1, local copies, waits for them, and re-layouts, shards(): ordered = bottom_source[order_rows] * row_mask  4.57 us
  transfers between devices with their start and end apart: 8, of which 8 were waited for; matrix products, arithmetic and copies ran while one was open for 0% of the time, Pallas kernels for 0%

profile of v1, /device:TPU:0, one launch (start us, length us, event | category | flops | bytes accessed | tf_op | source)
XLA Modules:
  0.0 181.1 jit_solution(529740205689723240)
XLA Ops:
  8.0 0.7 compare_select_fusion
  8.7 4.6 %gather_fusion = bf16[1024,256]{1,0:T(8,128)(2,1)S(1)} fusion(bf16[1024,256]{1,0:T(8,128)(2,1)} %param.11, s32[1024]{0:T(1024)S(1)} %broadcast_clamp_fusion), kind=kCustom, calls=%fused_computation | custom fusion | bytes 1052672 | tf_op jit(solution)/shard_map/gather | solution.py:55
  13.4 1.0 fusion.3
  14.4 0.8 copy-done.3
  15.2 0.3 convolution_bitcast_fusion.2
  15.5 0.1 copy.40
  15.6 0.8 fusion.45
  16.4 1.7 scatter_custom_fusion
  18.2 7.2 %all_gather.9 = bf16[448,256]{0,1:T(8,128)(2,1)S(1)} all-gather(bf16[448,64]{0,1:T(8,128)(2,1)S(1)} %copy-done.7), channel_id=1, replica_groups=mesh['rec'=2,'leaf'=4,'rhs'=2,'pan'=2] {'rhs','pan'}, dimensions={1}, use_global_device_ids=true | all-gather | bytes 286720 | tf_op jit(solution)/shard_map/all_gather | solution.py:64
  25.4 0.1 copy.52
  25.5 0.1 copy.53
  25.6 12.0 %all-gather.3.cloned.1.call-done = f32[1024,256]{1,0:T(8,128)} async-done(((f32[256,256]{1,0:T(8,128)}), f32[1024,256]{1,0:T(8,128)}) %all-gather.3.cloned.1.call-update) | async-done | bytes 1048592 | tf_op jit(solution)/shard_map/all_gather | solution.py:9
  37.7 1.3 reduce_sum.9
  39.0 0.2 convolution_convert_fusion.1
  39.3 0.2 fusion.8
  39.4 0.1 copy.41
  39.5 1.1 scatter_custom_fusion.1
  40.7 1.6 collective-permute-start
  42.3 6.8 %collective-permute-done = f32[256,256]{1,0:T(8,128)S(1)} collective-permute-done((f32[256,256]{1,0:T(8,128)S(1)}, f32[256,256]{1,0:T(8,128)S(1)}, u32[]{:S(2)}, u32[]{:S(2)}) %collective-permute-start) | collective-permute-done | bytes 262176 | tf_op jit(solution)/shard_map/ppermute | solution.py:18
  49.2 0.2 convolution_convert_fusion.2
  49.4 0.2 fusion.9
  49.6 0.1 copy.43
  49.7 1.1 scatter_custom_fusion.2
  50.8 1.6 collective-permute-start.1
  52.3 6.1 %collective-permute-done.1 = f32[256,256]{1,0:T(8,128)S(1)} collective-permute-done((f32[256,256]{1,0:T(8,128)S(1)}, f32[256,256]{1,0:T(8,128)S(1)}, u32[]{:S(2)}, u32[]{:S(2)}) %collective-permute-start.1) | collective-permute-done | bytes 262176 | tf_op jit(solution)/shard_map/ppermute | solution.py:18
  58.5 2.5 %collective-permute-start.2 = (f32[256,256]{1,0:T(8,128)S(1)}, f32[256,256]{1,0:T(8,128)S(1)}, u32[]{:S(2)}, u32[]{:S(2)}) collective-permute-start(f32[256,256]{1,0:T(8,128)S(1)} %add.115), channel_id=1, source_target_pairs={{0,8},{4,12},{8,0},{12,4},{1,9},{5,13},{9,1},{13,5},{2,10},{6,14},... | collective-permute-start | bytes 786440 | tf_op jit(solution)/shard_map/ppermute | solution.py:18
  61.0 10.8 %collective-permute-done.2 = f32[256,256]{1,0:T(8,128)S(1)} collective-permute-done((f32[256,256]{1,0:T(8,128)S(1)}, f32[256,256]{1,0:T(8,128)S(1)}, u32[]{:S(2)}, u32[]{:S(2)}) %collective-permute-start.2) | collective-permute-done | bytes 262176 | tf_op jit(solution)/shard_map/ppermute | solution.py:18
  71.8 0.4 convolution_bitcast_fusion.1
  72.2 0.6 collective-permute-start.3
  72.8 6.7 %collective-permute-done.3 = f32[256,256]{0,1:T(8,128)S(1)} collective-permute-done((f32[256,256]{0,1:T(8,128)S(1)}, f32[256,256]{0,1:T(8,128)S(1)}, u32[]{:S(2)}, u32[]{:S(2)}) %collective-permute-start.3) | collective-permute-done | bytes 262176 | tf_op jit(solution)/shard_map/ppermute | solution.py:18
  79.5 3.2 %collective-permute-start.4 = (f32[256,256]{0,1:T(8,128)S(1)}, f32[256,256]{0,1:T(8,128)S(1)}, u32[]{:S(2)}, u32[]{:S(2)}) collective-permute-start(f32[256,256]{0,1:T(8,128)S(1)} %add.117), channel_id=1, source_target_pairs={{0,8},{4,12},{8,0},{12,4},{1,9},{5,13},{9,1},{13,5},{2,10},{6,14},... | collective-permute-start | bytes 786440 | tf_op jit(solution)/shard_map/ppermute | solution.py:18
  82.7 11.6 %collective-permute-done.4 = f32[256,256]{0,1:T(8,128)S(1)} collective-permute-done((f32[256,256]{0,1:T(8,128)S(1)}, f32[256,256]{0,1:T(8,128)S(1)}, u32[]{:S(2)}, u32[]{:S(2)}) %collective-permute-start.4) | collective-permute-done | bytes 262176 | tf_op jit(solution)/shard_map/ppermute | solution.py:18
  94.4 0.1 copy.45
  94.5 0.8 gather_fusion.1
  95.3 0.3 convolution_bitcast_fusion
  95.7 0.7 collective-permute-start.5
  96.4 6.6 %collective-permute-done.5 = f32[256,256]{0,1:T(8,128)S(1)} collective-permute-done((f32[256,256]{0,1:T(8,128)S(1)}, f32[256,256]{0,1:T(8,128)S(1)}, u32[]{:S(2)}, u32[]{:S(2)}) %collective-permute-start.5) | collective-permute-done | bytes 262176 | tf_op jit(solution)/shard_map/ppermute | solution.py:18
  103.1 0.1 copy.46
  103.2 0.8 gather_fusion.2
  104.1 0.4 fusion.7
  104.4 0.1 copy.47
  104.5 0.8 gather_fusion.3
  105.4 2.6 %fusion.4 = bf16[1024,256]{0,1:T(8,128)(2,1)} fusion(bf16[1024,1024]{1,0:T(8,128)(2,1)S(1)} %copy-done, bf16[128,256]{1,0:T(8,128)(2,1)S(1)} %gather_fusion.3, bf16[128,1024]{1,0:T(8,128)(2,1)} %param.13, bf16[256,1024]{1,0:T(8,128)(2,1)S(1)} %copy-done.4, f32[1024]{0:T(1024)S(1)} %get-tuple-element.14), kind=kOutput, calls=%fused_computation.15 | convolution fusion | flops 605552640 | bytes 3477504 | tf_op jit(solution)/shard_map/ij,ic->jc/dot_general | solution.py:119
  108.0 1.2 copy.48
  109.3 5.1 %scatter_custom_fusion.3 = bf16[1024,256]{1,0:T(8,128)(2,1)S(1)} fusion(s32[1024]{0:T(1024)S(1)} %bitcast.57, bf16[1024,256]{1,0:T(8,128)(2,1)S(1)} %copy.48, bf16[]{:T(256)} %constant.57.clone.1), kind=kCustom, calls=%fused_computation.42 | custom fusion | bytes 524290 | tf_op jit(solution)/shard_map/scatter | solution.py:122
  114.4 1.9 %fusion.5 = f32[512,256]{0,1:T(8,128)S(1)} fusion(bf16[1024,256]{1,0:T(8,128)(2,1)S(1)} %scatter_custom_fusion.3, bf16[512,1024]{1,0:T(8,128)(2,1)} %param.14), kind=kOutput, calls=%fused_computation.17 | convolution fusion | flops 268566528 | bytes 2097152 | tf_op jit(solution)/shard_map/dot_general | solution.py:124
  116.3 1.0 copy.50
  117.3 56.9 %reduce-scatter.4.cloned.1.call-done = f32[32,256]{1,0:T(8,128)} async-done(((f32[512,256]{1,0:T(8,128)}), f32[32,256]{1,0:T(8,128)}) %reduce-scatter.4.cloned.1.call-update) | async-done | bytes 32784
  (36 shorter events, 0.5 us)
Async XLA Ops:
  7.2 6.2 %copy-start = (bf16[1024,1024]{1,0:T(8,128)(2,1)S(1)}, bf16[1024,1024]{1,0:T(8,128)(2,1)}, u32[]{:S(2)}) copy-start(bf16[1024,1024]{1,0:T(8,128)(2,1)} %param.12) | copy-start | bytes 6291460
  7.2 30.5 %all-gather.3.cloned.1.call-start = ((), (), s32[]{:S(2)}) async-start(), calls=%async_computation.1 | async-start | bytes 1310720 | tf_op jit(solution)/shard_map/all_gather | solution.py:9
  13.3 1.9 %copy-start.6 = (bf16[128,1024]{1,0:T(8,128)(2,1)S(1)}, bf16[128,1024]{1,0:T(8,128)(2,1)}, u32[]{:S(2)}) copy-start(bf16[128,1024]{1,0:T(8,128)(2,1)} %param.13) | copy-start | bytes 786436
  13.3 2.3 %copy-start.8 = (s32[1,128]{1,0:T(1,128)S(1)}, s32[1,128]{1,0:T(1,128)}, u32[]{:S(2)}) copy-start(s32[1,128]{1,0:T(1,128)} %param.17) | copy-start | bytes 1540
  13.4 4.8 %copy-start.7 = (bf16[448,64]{0,1:T(8,128)(2,1)S(1)}, bf16[448,64]{0,1:T(8,128)(2,1)}, u32[]{:S(2)}) copy-start(bf16[448,64]{0,1:T(8,128)(2,1)} %param.18) | copy-start | bytes 172036
  14.4 0.8 copy-start.3
  15.2 23.8 %copy-start.2 = (bf16[448,256]{1,0:T(8,128)(2,1)S(1)}, bf16[448,256]{1,0:T(8,128)(2,1)}, u32[]{:S(2)}) copy-start(bf16[448,256]{1,0:T(8,128)(2,1)} %param.19) | copy-start | bytes 688132
  15.5 23.8 %copy-start.5 = (bf16[128,384]{1,0:T(8,128)(2,1)S(1)}, bf16[128,384]{1,0:T(8,128)(2,1)}, u32[]{:S(2)}) copy-start(bf16[128,384]{1,0:T(8,128)(2,1)} %param.20) | copy-start | bytes 294916
  18.1 156.1 %reduce-scatter.4.cloned.1.call-start = ((), (), s32[]{:S(2)}) async-start(), calls=%async_computation.2 | async-start | bytes 557056
  40.7 8.5 %collective-permute-start = (f32[256,256]{1,0:T(8,128)S(1)}, f32[256,256]{1,0:T(8,128)S(1)}, u32[]{:S(2)}, u32[]{:S(2)}) collective-permute-start(f32[256,256]{1,0:T(8,128)S(1)} %add_dynamic-update-slice_fusion), channel_id=1, source_target_pairs={{0,4},{4,0},{8,12},{12,8},{1,5},{5,1},{9,13},{13,9},{2,6},{6,2},{1... | collective-permute-start | bytes 786440 | tf_op jit(solution)/shard_map/ppermute | solution.py:18
  50.8 7.7 %collective-permute-start.1 = (f32[256,256]{1,0:T(8,128)S(1)}, f32[256,256]{1,0:T(8,128)S(1)}, u32[]{:S(2)}, u32[]{:S(2)}) collective-permute-start(f32[256,256]{1,0:T(8,128)S(1)} %add_dynamic-update-slice_fusion.1), channel_id=1, source_target_pairs={{0,4},{4,0},{8,12},{12,8},{1,5},{5,1},{9,13},{13,9},{2,6},{6,2},{1... | collective-permute-start | bytes 786440 | tf_op jit(solution)/shard_map/ppermute | solution.py:18
  58.5 13.3 %collective-permute-start.2 = (f32[256,256]{1,0:T(8,128)S(1)}, f32[256,256]{1,0:T(8,128)S(1)}, u32[]{:S(2)}, u32[]{:S(2)}) collective-permute-start(f32[256,256]{1,0:T(8,128)S(1)} %add.115), channel_id=1, source_target_pairs={{0,8},{4,12},{8,0},{12,4},{1,9},{5,13},{9,1},{13,5},{2,10},{6,14},... | collective-permute-start | bytes 786440 | tf_op jit(solution)/shard_map/ppermute | solution.py:18
  72.2 7.3 %collective-permute-start.3 = (f32[256,256]{0,1:T(8,128)S(1)}, f32[256,256]{0,1:T(8,128)S(1)}, u32[]{:S(2)}, u32[]{:S(2)}) collective-permute-start(f32[256,256]{0,1:T(8,128)S(1)} %convolution_bitcast_fusion.1), channel_id=1, source_target_pairs={{0,4},{4,0},{8,12},{12,8},{1,5},{5,1},{9,13},{13,9},{2,6},{6,2},{1... | collective-permute-start | bytes 786440 | tf_op jit(solution)/shard_map/ppermute | solution.py:18
  79.5 14.8 %collective-permute-start.4 = (f32[256,256]{0,1:T(8,128)S(1)}, f32[256,256]{0,1:T(8,128)S(1)}, u32[]{:S(2)}, u32[]{:S(2)}) collective-permute-start(f32[256,256]{0,1:T(8,128)S(1)} %add.117), channel_id=1, source_target_pairs={{0,8},{4,12},{8,0},{12,4},{1,9},{5,13},{9,1},{13,5},{2,10},{6,14},... | collective-permute-start | bytes 786440 | tf_op jit(solution)/shard_map/ppermute | solution.py:18
  94.3 11.0 %copy-start.4 = (bf16[256,1024]{1,0:T(8,128)(2,1)S(1)}, bf16[256,1024]{1,0:T(8,128)(2,1)}, u32[]{:S(2)}) copy-start(bf16[256,1024]{1,0:T(8,128)(2,1)} %copy-done.3) | copy-start | bytes 1572868
  95.7 7.4 %collective-permute-start.5 = (f32[256,256]{0,1:T(8,128)S(1)}, f32[256,256]{0,1:T(8,128)S(1)}, u32[]{:S(2)}, u32[]{:S(2)}) collective-permute-start(f32[256,256]{0,1:T(8,128)S(1)} %convolution_bitcast_fusion), channel_id=1, source_target_pairs={{0,4},{4,0},{8,12},{12,8},{1,5},{5,1},{9,13},{13,9},{2,6},{6,2},{1... | collective-permute-start | bytes 786440 | tf_op jit(solution)/shard_map/ppermute | solution.py:18
  114.3 59.9 %copy-start.1 = (bf16[1024,256]{1,0:T(8,128)(2,1)}, bf16[1024,256]{1,0:T(8,128)(2,1)S(1)}, u32[]{:S(2)}) copy-start(bf16[1024,256]{1,0:T(8,128)(2,1)S(1)} %scatter_custom_fusion.3) | copy-start | bytes 1572868
Sparse Core Ops, SparseCore 0:
  18.2 19.4 all-gather.2
  117.4 56.7 reduce-scatter.3
